TPU v7x, 512 devices: a whole 4x8x8 slice. The times are simulated.
512 devices in a mesh: hour: 64 (over z_hi, y, core), bus: 8 (over x, z_lo).
Axes of the slice: x: 4, y: 8, z: 8 (z_hi: 4, z_lo: 2; z = z_hi * 2 + z_lo), core: 2. Of those that a mesh axis runs over, the one named last changes fastest.
Arguments:
- line_sensitivity: float32 [2000, 3072], P('bus'), may hold values from -0.125 to 0.125
- demand: float32 [2000, 8192], P('bus', 'hour'), may hold values from 0.05 to 1
- unit_cost: float32 [2000, 8192], P('bus', 'hour'), may hold values from 0.1 to 2
- output_limit: float32 [2000], P('bus'), may hold values from 0.2 to 2
- output_start: float32 [2000, 8192], P('bus', 'hour'), may hold values from 0 to 1
- line_limit: float32 [3072], replicated, may hold values from 0.1 to 1
- line_dual: float32 [3072, 8192], P('bus', 'hour'), may hold values from -3 to 3
- storage_bus: int32 [2000], P('bus'), may hold values from 0 to 1999, as said below
- charge_limit: float32 [2000], P('bus'), may hold values from 0.05 to 0.5
- charge_start: float32 [2000, 8192], P('bus', 'hour'), may hold values from -0.2 to 0.2
- level_start: float32 [2000], P('bus'), may hold values from 1 to 6
- level_limit: float32 [2000], P('bus'), may hold values from 3 to 30
- level_dual: float32 [2000, 8192], P('bus', 'hour'), may hold values from -0.2 to 0.2
- balance_dual: float32 [8192], P('hour'), may hold values from -3 to 3
Outputs:
- generation: float32 [2000, 8192], P('bus', 'hour')
- charging: float32 [2000, 8192], P('bus', 'hour')
- storage_level: float32 [2000, 8192], P('bus', 'hour')
- line_dual_next: float32 [3072, 8192], P('bus', 'hour')
- level_dual_next: float32 [2000, 8192], P('bus', 'hour')
- balance_dual_next: float32 [8192], P('hour')
Inputs may be any that keep to these rules, and one draw needn't show every extreme that they name: `storage_bus`: storage s is connected to a bus b with b // 250 equal to s // 250; storage 0 is at bus 0 and storage 2000 - 1 at bus 2000 - 1.
All inputs are finite; a program needn't handle non-finite values.
Results may differ from a plain program's by a relative error of at most 0.00011.
Values sent between devices are 32-bit elements; how exact they have to be, the bound alone decides.
A program may use at most 64 MiB of HBM per device.

v0:
```python
import jax
import jax.numpy as jnp
from jax import lax
from jax.experimental import pallas as pl
from jax.experimental.pallas import tpu as pltpu
from jax.sharding import PartitionSpec as P

B = 2000
S = 2000
ITERS = 2
HOURS = 8192
NB = 250
NP = 256
HD = 128
LD = 384
NL = 3072
NX = 4
NY = 8
NZ = 4
ROW = 8
MESH = pl.DeviceIdType.MESH
HIGHEST = lax.Precision.HIGHEST
F32 = jnp.float32
BF16 = jnp.bfloat16
PEERS = ((2, 1), (1, 1), (3, 1), (2, 0), (1, 0), (3, 0), (0, 1))
PIECE = 32
ARRAYS = 14


def dot(a, b, dims, precision=None):
    return lax.dot_general(a, b, (dims, ((), ())), precision=precision, preferred_element_type=F32)


def halves(value):
    high = value.astype(BF16)
    return high, (value - high.astype(F32)).astype(BF16)


def column(row, count):
    return jnp.broadcast_to(row, (HD, count)).T


def dot_exact(a, b, dims):
    if a.dtype == BF16:
        high, low = halves(b)
        return dot(a, high, dims) + dot(a, low, dims)
    high, low = halves(a)
    return dot(high, b, dims) + dot(low, b, dims)


class Place:
    def __init__(self):
        self.hour = lax.axis_index("hour")
        self.bus = lax.axis_index("bus")
        self.x = self.bus // 2
        self.z = lax.rem(self.bus, 2)
        self.high, self.y, self.core = self.hour // 16, lax.rem(self.hour // 2, NY), lax.rem(self.hour, 2)

    def block(self, dx, dz):
        return lax.rem(self.x + dx + NX, NX) * 2 + lax.rem(self.z + dz, 2)

    def bus_peer(self, dx, dz):
        return (self.hour, self.block(dx, dz))

    def y_peer(self, d):
        return (self.high * 16 + lax.rem(self.y + d + NY, NY) * 2 + self.core, self.bus)

    def z_peer(self, d):
        return (lax.rem(self.high + d, NZ) * 16 + self.y * 2 + self.core, self.bus)

    def core_peer(self):
        return (self.hour + 1 - 2 * self.core, self.bus)


class Sends:
    def __init__(self):
        self.groups = []

    def start(self, src, dst, send_sem, recv_sem, device):
        pltpu.make_async_remote_copy(
            src_ref=src, dst_ref=dst, send_sem=send_sem, recv_sem=recv_sem, device_id=device, device_id_type=MESH
        ).start()

    def group(self, ref, send_sem):
        self.groups.append((ref, send_sem))

    def finish(self):
        for ref, sem in self.groups:
            pltpu.make_async_copy(ref, ref, sem).wait()


def arrived(ref, recv_sem):
    pltpu.make_async_copy(ref, ref, recv_sem).wait()


class Gather:
    def __init__(self, place, sends, buf, rows, cut, send_sem, recv_sem):
        h = rows // 2
        self.place, self.sends, self.buf = place, sends, buf
        self.send_sem, self.recv_sem = send_sem, recv_sem
        right, left, across = (1, 0), (3, 0), (0, 1)
        self.plan = {
            "r1": (right, (0, 0), 0, h),
            "r2": (right, (0, 0), h, rows),
            "r3": (right, (3, 0), 0, h),
            "r4": (right, (0, 1), cut, rows),
            "r5": (right, (3, 1), 0, h),
            "l1": (left, (0, 0), h, rows),
            "l2": (left, (0, 0), 0, h),
            "l3": (left, (1, 0), h, rows),
            "l4": (left, (0, 1), 0, rows - cut),
            "l5": (left, (1, 1), h, rows),
            "z1": (across, (0, 0), 0, h),
            "z2": (across, (0, 0), h, rows),
            "z3": (across, (3, 0), 0, h),
            "z4": (across, (1, 0), h, rows),
            "z5": (across, (3, 0), h, cut),
            "z6": (across, (1, 0), rows - cut, h),
        }
        self.number = {key: i for i, key in enumerate(self.plan)}

    def send(self, *keys):
        for key in keys:
            to, block, first, last = self.plan[key]
            ref = self.buf.at[self.place.block(*block), pl.ds(first, last - first)]
            i = self.number[key]
            self.sends.start(ref, ref, self.send_sem, self.recv_sem.at[i], self.place.bus_peer(*to))

    def wait(self, *keys):
        for key in keys:
            to, block, first, last = self.plan[key]
            at = self.place.block((block[0] - to[0]) % NX, (block[1] + to[1]) % 2)
            ref = self.buf.at[at, pl.ds(first, last - first)]
            i = self.number[key]
            arrived(ref, self.recv_sem.at[i])

    def begin(self):
        self.send("r1", "l1", "z1", "r2", "l2", "z2")
        self.sends.group(self.buf.at[pl.ds(0, 7)], self.send_sem)

    def run(self, use, beside):
        block = self.place.block
        self.wait("r1")
        self.send("r3", "z3")
        self.wait("l1")
        self.send("l3", "z4")
        beside(1)
        self.wait("r2")
        self.send("z5")
        self.wait("l2")
        self.send("z6")
        self.wait("z1")
        self.send("l4")
        self.wait("z2")
        self.send("r4")
        beside(2)
        use(block(0, 0))
        use(block(3, 0))
        self.wait("z3")
        self.send("r5")
        self.wait("z4")
        self.send("l5")
        beside(3)
        use(block(1, 0))
        use(block(0, 1))
        self.wait("r3", "l3")
        beside(4)
        use(block(2, 0))
        self.wait("z5", "r4")
        use(block(3, 1))
        self.wait("z6", "l4")
        use(block(1, 1))
        beside(5)
        self.wait("r5", "l5")
        use(block(2, 1))


class Columns:
    def __init__(self, place, sends, buf, piece, bus_send, bus_recv, ring_send, ring_recv):
        self.place, self.sends, self.buf, self.piece = place, sends, buf, piece
        self.bus_send, self.bus_recv = bus_send, bus_recv
        self.ring_send, self.ring_recv = ring_send, ring_recv

    def eighth(self):
        return lax.rem(self.place.y, 4) * 2 + self.place.core

    def rows(self, dy, part=None, other=False):
        core = 1 - self.place.core if other else self.place.core
        at = (lax.rem(self.place.y + dy + NY, 4) * 2 + core) * PIECE
        if part is None:
            return self.buf.at[pl.ds(1, 7), pl.ds(pl.multiple_of(at, PIECE), PIECE)]
        half = PIECE // 2
        return self.buf.at[pl.ds(1, 7), pl.ds(pl.multiple_of(at + part * half, half), half)]

    def begin(self):
        place = self.place
        at = pl.multiple_of(self.eighth() * PIECE, PIECE)
        for k in range(1, 8):
            to = lax.rem(place.bus + k, 8)
            src = self.piece.at[:, pl.ds(pl.multiple_of(to * LD, HD), LD)]
            dst = self.buf.at[8 - k, pl.ds(at, PIECE)]
            self.sends.start(src, dst, self.bus_send, self.bus_recv, (place.hour, to))

        self.sends.group(self.rows(0), self.bus_send)
        self.sends.group(self.buf.at[pl.ds(1, 7), pl.ds(0, 7 * PIECE)], self.ring_send)

    def pass_on(self, i, ref, device):
        self.sends.start(ref, ref, self.ring_send, self.ring_recv.at[i], device)

    def came(self, i, ref):
        arrived(ref, self.ring_recv.at[i])

    def fetched(self):
        place = self.place
        arrived(self.rows(0), self.bus_recv)
        up, down = place.y_peer(1), place.y_peer(-1)
        self.pass_on(0, self.rows(0, 0), up)
        self.pass_on(1, self.rows(0, 1), down)
        self.pass_on(2, self.rows(0, 1), up)
        self.pass_on(3, self.rows(0, 0), down)
        self.pass_on(6, self.rows(0), place.core_peer())

    def first_halves(self):
        self.came(0, self.rows(-1, 0))
        self.pass_on(4, self.rows(-1, 0), self.place.y_peer(1))
        self.came(1, self.rows(1, 1))
        self.pass_on(5, self.rows(1, 1), self.place.y_peer(-1))

    def second_halves(self):
        self.came(2, self.rows(-1, 1))
        self.pass_on(7, self.rows(-1), self.place.core_peer())
        self.came(3, self.rows(1, 0))
        self.pass_on(8, self.rows(1), self.place.core_peer())

    def far_halves(self):
        self.came(4, self.rows(2, 0))
        self.came(5, self.rows(2, 1))
        self.pass_on(9, self.rows(2), self.place.core_peer())

    def end(self):
        for i, dy in ((6, 0), (7, -1), (8, 1), (9, 2)):
            self.came(i, self.rows(dy, other=True))


class Prefix:
    SLOTS = 2 + NY + NZ

    def __init__(self, place, sends, buf, send_sem, recv_sem):
        self.place, self.sends, self.buf = place, sends, buf
        self.send_sem, self.recv_sem = send_sem, recv_sem

    def give(self, stage, slot, devices):
        ref = self.buf.at[slot]
        for device in devices:
            self.sends.start(ref, ref, self.send_sem.at[stage], self.recv_sem.at[stage], device)
        self.sends.group(self.buf.at[pl.ds(0, len(devices))], self.send_sem.at[stage])

    def take(self, stage, count):
        arrived(self.buf.at[pl.ds(0, count)], self.recv_sem.at[stage])

    def begin(self, value):
        place = self.place
        self.buf[place.core] = dot(jnp.ones((ROW, HD), F32), value, ((1,), (1,)), HIGHEST)[0:1]
        self.give(0, place.core, [place.core_peer()])

    def over_y(self):
        place = self.place
        self.take(0, 1)
        self.buf[2 + place.y] = self.buf[0] + self.buf[1]
        self.give(1, 2 + place.y, [place.y_peer(d) for d in (4, 3, 5, 2, 6, 1, 7)])

    def over_z(self):
        place = self.place
        self.take(1, NY - 1)
        total = self.buf[2]
        for i in range(1, NY):
            total = total + self.buf[2 + i]
        self.buf[2 + NY + place.high] = total
        self.give(2, 2 + NY + place.high, [place.z_peer(d) for d in (2, 1, 3)])

    def end(self, reverse):
        place = self.place
        self.take(2, NZ - 1)
        row = jnp.zeros((1, NP), F32)
        for base, count, mine in ((0, 2, place.core), (2, NY, place.y), (2 + NY, NZ, place.high)):
            for i in range(count):
                reached = (mine < i) if reverse else (mine > i)
                row = row + self.buf[base + i] * jnp.where(reached, 1.0, 0.0)
        return column(row, NP)[0:NB]


def kernel(*refs):
    (sens_h, demand_h, cost_h, olim_h, gen_h, llim_h, line_h, sbus_h, clim_h, chg_h, lstart_h, llev_h, ldual_h, bal_h) = refs[:14]
    (gen_o, chg_o, level_o, line_o, ldual_o, bal_o) = refs[14:20]
    (sens, demand, cost, olim_r, gen, llim_r, sbus_r, clim_r, chg, lstart_r, llev_r, ldual, bal) = refs[20:33]
    (shi, slo, tail, lines1, lines2, inj1, inj2, cols, chi, clo, piece, acc, pad_l, pad_c, pad_i, hot, hot_t, spread, level_v, line_v, pre) = refs[33:54]
    (in_sem, out_sem, g1s, g1r, g2s, g2r, i1s, i1r, i2s, i2r, cbs, cbr, crs, crr, ps, pr) = refs[54:]
    place = Place()
    sends = Sends()

    ins = {}
    for i, (src, dst) in enumerate(
        (
            (line_h, lines1.at[place.bus]),
            (ldual_h, ldual),
            (sens_h, sens),
            (llim_h, llim_r),
            (sbus_h, sbus_r),
            (olim_h, olim_r),
            (clim_h, clim_r),
            (lstart_h, lstart_r),
            (llev_h, llev_r),
            (bal_h, bal),
            (demand_h, demand),
            (cost_h, cost),
            (gen_h, gen),
            (chg_h, chg),
        )
    ):
        ins[i] = pltpu.make_async_copy(src, dst, in_sem.at[i])
        ins[i].start()

    barrier = pltpu.get_barrier_semaphore()
    partners = [place.bus_peer(*d) for d in PEERS]
    partners += [place.core_peer()]
    partners += [place.y_peer(d) for d in range(1, NY)]
    partners += [place.z_peer(d) for d in range(1, NZ)]
    for device in partners:
        pl.semaphore_signal(barrier, inc=1, device_id=device, device_id_type=MESH)

    zeros = jnp.zeros((NP - NB, HD), F32)
    for ref in (pad_l, pad_c, pad_i):
        ref[NB:NP, :] = zeros
    acc[...] = jnp.zeros((NP, HD), F32)
    ins[0].wait()
    pl.semaphore_wait(barrier, len(partners))

    gather1 = Gather(place, sends, lines1, LD, 256, g1s, g1r)
    gather1.begin()
    prefixes = [Prefix(place, sends, pre.at[k], ps.at[k], pr.at[k]) for k in range(4)]
    ins[1].wait()
    pad_l[0:NB, :] = ldual[...]
    prefixes[0].begin(pad_l[...])
    ins[2].wait()
    tail[0:26, :] = sens[224:NB, :]
    tail[26:32, :] = jnp.zeros((6, NL), F32)
    columns = Columns(place, sends, cols, piece, cbs, cbr, crs, crr)
    eighth = columns.eighth()

    @pl.when(eighth < 7)
    def _():
        piece[...] = sens[pl.ds(pl.multiple_of(eighth * PIECE, PIECE), PIECE), :]

    @pl.when(eighth == 7)
    def _():
        piece[...] = tail[...]

    columns.begin()
    prefixes[0].over_y()
    first_line = pl.multiple_of(place.bus * LD, HD)
    cols[0, 0:224, :] = sens[0:224, pl.ds(first_line, LD)]
    cols[0, 224:NP, :] = tail[:, pl.ds(first_line, LD)]

    @pl.loop(0, 14)
    def _(i):
        rows = pl.ds(pl.multiple_of(i * 16, 16), 16)
        shi[rows, :], slo[rows, :] = halves(sens[rows, :])

    shi[224:NP, :], slo[224:NP, :] = halves(tail[...])

    for i in range(3, ARRAYS):
        ins[i].wait()

    olim = column(olim_r[0:1, :], NB)
    clim = column(clim_r[0:1, :], NB)
    lstart = column(lstart_r[0:1, :], NB)
    llev = column(llev_r[0:1, :], NB)
    llim = column(llim_r[0:1, pl.ds(first_line, LD)], LD)
    at_bus = lax.broadcasted_iota(jnp.int32, (NP, NB), 0)
    local = sbus_r[0:1, :] - place.bus * NB
    spread[...] = jnp.zeros((NP, NP), F32)
    spread[:, 0:NB] = (at_bus == local).astype(F32)
    hot[...] = spread[...].astype(BF16)
    hot_t[...] = spread[...].T.astype(BF16)
    hour_at = lax.broadcasted_iota(jnp.int32, (HD, HD), 0)
    hour_to = lax.broadcasted_iota(jnp.int32, (HD, HD), 1)
    until = (hour_at <= hour_to).astype(F32).astype(BF16)
    since = (hour_at >= hour_to).astype(F32).astype(BF16)
    hour_pos = (place.hour * HD + lax.broadcasted_iota(jnp.int32, (1, HD), 1)).astype(F32)
    step = 1.0 / (float(HOURS) - hour_pos + 4.0)

    def add_adjoint(lines):
        def use(block):
            cols = pl.ds(pl.multiple_of(block * LD, HD), LD)
            high, low = halves(lines[block])
            sh = shi[:, cols]
            acc[...] += dot(sh, high, ((1,), (0,))) + (dot(slo[:, cols], high, ((1,), (0,))) + dot(sh, low, ((1,), (0,))))

        return use

    def primal(balance, later, prefix):
        adjoint = acc[0:NB, :]
        at_storage = dot_exact(hot_t[...], acc[...], ((1,), (0,)))[0:NB]
        generation, charging = gen[...], chg[...]
        charge_new = jnp.clip(charging - step * (later - at_storage - balance), -clim, clim)
        pad_c[0:NB, :] = 2.0 * charge_new - charging
        prefix.begin(pad_c[...])
        output_new = jnp.clip(generation - 0.25 * (cost[...] + adjoint + balance), 0.0, olim)
        gen[...] = output_new
        chg[...] = charge_new
        return 2.0 * output_new - generation - demand[...]

    def inject(output_bar, buf, send_sem, recv_sem, prefix):
        pad_i[0:NB, :] = output_bar - dot_exact(hot[...], pad_c[...], ((1,), (0,)))[0:NB]
        prefix.over_y()
        buf[place.bus] = pad_i[...].T
        gather = Gather(place, sends, buf, HD, 88, send_sem, recv_sem)
        gather.begin()
        return gather

    def split_columns():
        for k in range(8):
            chi[k], clo[k] = halves(cols[k])

    def flows_of(gather, buf, beside):
        sums = [jnp.zeros((HD, LD), F32), jnp.zeros((HD, NP), F32)]

        def use(block):
            k = lax.rem(block - place.bus + 8, 8)
            injection = buf[block]
            high, low = halves(injection)
            ch = chi[k]
            sums[0] += dot(high, ch, ((1,), (0,))) + (dot(low, ch, ((1,), (0,))) + dot(high, clo[k], ((1,), (0,))))
            sums[1] += injection

        gather.run(use, beside)
        total = dot(jnp.ones((ROW, NP), F32), sums[1], ((1,), (1,)), HIGHEST)
        return sums[0].T, total[0:1]

    def line_step(line, flows):
        raised = 4.0 * line + flows
        return 0.25 * (raised - jnp.clip(raised, -llim, llim))

    def level_step(carried):
        level = lstart + carried + dot_exact(pad_c[...], until, ((1,), (0,)))[0:NB]
        raised = 4.0 * pad_l[0:NB, :] + level
        pad_l[0:NB, :] = 0.25 * (raised - jnp.clip(raised, 0.0, llev))
        return level

    def later_of(carried):
        return carried + dot_exact(pad_l[...], since, ((1,), (0,)))[0:NB]

    def beside(at):
        if at == 2:
            prefixes[0].over_z()
            columns.fetched()
        if at == 5:
            columns.first_halves()

    gather1.run(add_adjoint(lines1), beside)
    balance = bal[0:1, :]
    output_bar = primal(balance, later_of(prefixes[0].end(True)), prefixes[1])
    gather = inject(output_bar, inj1, i1s, i1r, prefixes[1])
    columns.second_halves()

    def beside(at):
        if at == 1:
            columns.far_halves()
        if at == 2:
            prefixes[1].over_z()
            columns.end()
            split_columns()

    flows, total = flows_of(gather, inj1, beside)
    lines2[place.bus] = line_step(lines1[place.bus], flows)
    gather2 = Gather(place, sends, lines2, LD, 256, g2s, g2r)
    gather2.begin()
    balance = balance + total * (1.0 / float(B + S))
    level_step(prefixes[1].end(False))
    prefixes[2].begin(pad_l[...])
    acc[...] = jnp.zeros((NP, HD), F32)
    prefixes[2].over_y()

    def beside(at):
        if at == 3:
            prefixes[2].over_z()

    gather2.run(add_adjoint(lines2), beside)
    output_bar = primal(balance, later_of(prefixes[2].end(True)), prefixes[3])
    gather = inject(output_bar, inj2, i2s, i2r, prefixes[3])
    outs = [pltpu.make_async_copy(gen, gen_o, out_sem.at[0]), pltpu.make_async_copy(chg, chg_o, out_sem.at[1])]
    outs[0].start()
    outs[1].start()
    flows, total = flows_of(gather, inj2, lambda at: prefixes[3].over_z() if at == 2 else None)
    line_v[...] = line_step(lines2[place.bus], flows)
    bal[0:1, :] = balance + total * (1.0 / float(B + S))
    outs.append(pltpu.make_async_copy(line_v, line_o, out_sem.at[2]))
    outs.append(pltpu.make_async_copy(bal, bal_o, out_sem.at[3]))
    outs[2].start()
    outs[3].start()
    level_v[...] = level_step(prefixes[3].end(False))
    ldual[...] = pad_l[0:NB, :]
    outs.append(pltpu.make_async_copy(level_v, level_o, out_sem.at[4]))
    outs.append(pltpu.make_async_copy(ldual, ldual_o, out_sem.at[5]))
    outs[4].start()
    outs[5].start()
    for copy in outs:
        copy.wait()
    sends.finish()


def store(*refs):
    copies = [pltpu.make_async_copy(refs[i], refs[6 + i], refs[12].at[i]) for i in range(6)]
    for copy in copies:
        copy.start()
    for copy in copies:
        copy.wait()


def body(
    line_sensitivity,
    demand,
    unit_cost,
    output_limit,
    output_start,
    line_limit,
    line_dual,
    storage_bus,
    charge_limit,
    charge_start,
    level_start,
    level_limit,
    level_dual,
    balance_dual,
):
    anywhere = pl.BlockSpec(memory_space=pl.ANY)
    block = jax.ShapeDtypeStruct((NB, HD), F32)
    vm = pltpu.VMEM
    dma = pltpu.SemaphoreType.DMA
    scratch = [
        vm((NB, NL), F32),
        vm((NB, HD), F32),
        vm((NB, HD), F32),
        vm((1, NB), F32),
        vm((NB, HD), F32),
        vm((1, NL), F32),
        vm((1, NB), jnp.int32),
        vm((1, NB), F32),
        vm((NB, HD), F32),
        vm((1, NB), F32),
        vm((1, NB), F32),
        vm((NB, HD), F32),
        vm((1, HD), F32),
        vm((NP, NL), BF16),
        vm((NP, NL), BF16),
        vm((PIECE, NL), F32),
        vm((8, LD, HD), F32),
        vm((8, LD, HD), F32),
        vm((8, HD, NP), F32),
        vm((8, HD, NP), F32),
        vm((8, NP, LD), F32),
        vm((8, NP, LD), BF16),
        vm((8, NP, LD), BF16),
        vm((PIECE, NL), F32),
        vm((NP, HD), F32),
        vm((NP, HD), F32),
        vm((NP, HD), F32),
        vm((NP, HD), F32),
        vm((NP, NP), BF16),
        vm((NP, NP), BF16),
        vm((NP, NP), F32),
        vm((NB, HD), F32),
        vm((LD, HD), F32),
        vm((4, Prefix.SLOTS, 1, NP), F32),
        dma((ARRAYS,)),
        dma((6,)),
        dma,
        dma((16,)),
        dma,
        dma((16,)),
        dma,
        dma((16,)),
        dma,
        dma((16,)),
        dma,
        dma,
        dma,
        dma((10,)),
        dma((4, 3)),
        dma((4, 3)),
    ]
    shapes = (block, block, block, jax.ShapeDtypeStruct((LD, HD), F32), block, jax.ShapeDtypeStruct((1, HD), F32))
    results = pl.pallas_call(
        kernel,
        out_shape=tuple(pltpu.VMEM(shape.shape, F32) for shape in shapes),
        in_specs=[anywhere] * ARRAYS,
        out_specs=[anywhere] * 6,
        scratch_shapes=scratch,
        compiler_params=pltpu.CompilerParams(collective_id=0, has_side_effects=True, vmem_limit_bytes=56 * 1024 * 1024),
    )(
        line_sensitivity,
        demand,
        unit_cost,
        output_limit.reshape(1, NB),
        output_start,
        line_limit.reshape(1, NL),
        line_dual,
        storage_bus.reshape(1, NB),
        charge_limit.reshape(1, NB),
        charge_start,
        level_start.reshape(1, NB),
        level_limit.reshape(1, NB),
        level_dual,
        balance_dual.reshape(1, HD),
    )
    generation, charging, level, line, dual, balance = pl.pallas_call(
        store,
        out_shape=shapes,
        in_specs=[anywhere] * 6,
        out_specs=[anywhere] * 6,
        scratch_shapes=[dma((6,))],
        compiler_params=pltpu.CompilerParams(vmem_limit_bytes=32 * 1024 * 1024),
    )(*[pltpu.with_memory_space_constraint(result, pltpu.VMEM) for result in results])
    return generation, charging, level, line, dual, balance.reshape(HD)


def solution(mesh):
    both = P("bus", "hour")
    return jax.shard_map(
        body,
        mesh=mesh,
        in_specs=(
            P("bus", None),
            both,
            both,
            P("bus"),
            both,
            P(),
            both,
            P("bus"),
            P("bus"),
            both,
            P("bus"),
            P("bus"),
            both,
            P("hour"),
        ),
        out_specs=(both, both, both, both, both, P("hour")),
        check_vma=False,
    )
```

profile of v0, /device:TPU:1, one launch (start us, length us, event | category | flops | bytes accessed | tf_op | source)
XLA Modules:
  0.0 78.9 jit_solution(8538787417739445124)
XLA Ops:
  0.6 77.4 %shard_map.181 = (f32[250,128]{1,0:T(8,128)S(1)}, f32[250,128]{1,0:T(8,128)S(1)}, f32[250,128]{1,0:T(8,128)S(1)}, f32[384,128]{1,0:T(8,128)S(1)}, f32[250,128]{1,0:T(8,128)S(1)}, /*index=5*/f32[1,128]{1,0:T(1,128)S(1)}) custom-call(f32[250,3072]{1,0:T(8,128)} %refs_0_.1, f32[250,128]{1,0:T(8,128)} %refs_1_.1, f32[250,128]{1,0:T(8,128)} %refs_2_.1, ...), custom_call_target="tpu_custom_call" | custom-call | tf_op jit(solution)/shard_map/pallas_call | solution.py:593
  78.0 0.9 %shard_map.182 = (f32[250,128]{1,0:T(8,128)}, f32[250,128]{1,0:T(8,128)}, f32[250,128]{1,0:T(8,128)}, f32[384,128]{1,0:T(8,128)}, f32[250,128]{1,0:T(8,128)}, /*index=5*/f32[1,128]{1,0:T(1,128)}) custom-call(f32[250,128]{1,0:T(8,128)S(1)} %get-tuple-element.18.refs_0_, f32[250,128]{1,0:T(8,128)S(1)} %get-tuple-element.19.refs_1_, ...), custom_call_target="tpu_custom_call" | custom-call | tf_op jit(solution)/shard_map/pallas_call | solution.py:616
where the time goes:
time: 79.1 us; the launch traced here: 78.9 us
  Pallas kernels  78.3 us (99%)
    pallas_call x1, Pallas kernels, body(): pl.pallas_call(kernel, out_shape=tuple((pltpu.VMEM(shape.shape, F32) for...  77.4 us

commit v1 on v0

--- a/solution.py
+++ b/solution.py
@@ -293,8 +293,8 @@
     (sens_h, demand_h, cost_h, olim_h, gen_h, llim_h, line_h, sbus_h, clim_h, chg_h, lstart_h, llev_h, ldual_h, bal_h) = refs[:14]
     (gen_o, chg_o, level_o, line_o, ldual_o, bal_o) = refs[14:20]
     (sens, demand, cost, olim_r, gen, llim_r, sbus_r, clim_r, chg, lstart_r, llev_r, ldual, bal) = refs[20:33]
-    (shi, slo, tail, lines1, lines2, inj1, inj2, cols, chi, clo, piece, acc, pad_l, pad_c, pad_i, hot, hot_t, spread, level_v, line_v, pre) = refs[33:54]
-    (in_sem, out_sem, g1s, g1r, g2s, g2r, i1s, i1r, i2s, i2r, cbs, cbr, crs, crr, ps, pr) = refs[54:]
+    (shi, slo, tail, lines1, lines2, inj1, inj2, cols, chi, clo, piece, acc, pad_l, pad_c, pad_i, hot, hot_t, spread, pre) = refs[33:52]
+    (in_sem, g1s, g1r, g2s, g2r, i1s, i1r, i2s, i2r, cbs, cbr, crs, crr, ps, pr) = refs[52:]
     place = Place()
     sends = Sends()
 
@@ -335,7 +335,7 @@
     ins[0].wait()
     pl.semaphore_wait(barrier, len(partners))
 
-    gather1 = Gather(place, sends, lines1, LD, 256, g1s, g1r)
+    gather1 = Gather(place, sends, lines1, LD, 208, g1s, g1r)
     gather1.begin()
     prefixes = [Prefix(place, sends, pre.at[k], ps.at[k], pr.at[k]) for k in range(4)]
     ins[1].wait()
@@ -414,7 +414,7 @@
         pad_i[0:NB, :] = output_bar - dot_exact(hot[...], pad_c[...], ((1,), (0,)))[0:NB]
         prefix.over_y()
         buf[place.bus] = pad_i[...].T
-        gather = Gather(place, sends, buf, HD, 88, send_sem, recv_sem)
+        gather = Gather(place, sends, buf, HD, 72, send_sem, recv_sem)
         gather.begin()
         return gather
 
@@ -473,7 +473,7 @@
 
     flows, total = flows_of(gather, inj1, beside)
     lines2[place.bus] = line_step(lines1[place.bus], flows)
-    gather2 = Gather(place, sends, lines2, LD, 256, g2s, g2r)
+    gather2 = Gather(place, sends, lines2, LD, 208, g2s, g2r)
     gather2.begin()
     balance = balance + total * (1.0 / float(B + S))
     level_step(prefixes[1].end(False))
@@ -488,24 +488,13 @@
     gather2.run(add_adjoint(lines2), beside)
     output_bar = primal(balance, later_of(prefixes[2].end(True)), prefixes[3])
     gather = inject(output_bar, inj2, i2s, i2r, prefixes[3])
-    outs = [pltpu.make_async_copy(gen, gen_o, out_sem.at[0]), pltpu.make_async_copy(chg, chg_o, out_sem.at[1])]
-    outs[0].start()
-    outs[1].start()
+    gen_o[...] = gen[...]
+    chg_o[...] = chg[...]
     flows, total = flows_of(gather, inj2, lambda at: prefixes[3].over_z() if at == 2 else None)
-    line_v[...] = line_step(lines2[place.bus], flows)
-    bal[0:1, :] = balance + total * (1.0 / float(B + S))
-    outs.append(pltpu.make_async_copy(line_v, line_o, out_sem.at[2]))
-    outs.append(pltpu.make_async_copy(bal, bal_o, out_sem.at[3]))
-    outs[2].start()
-    outs[3].start()
-    level_v[...] = level_step(prefixes[3].end(False))
-    ldual[...] = pad_l[0:NB, :]
-    outs.append(pltpu.make_async_copy(level_v, level_o, out_sem.at[4]))
-    outs.append(pltpu.make_async_copy(ldual, ldual_o, out_sem.at[5]))
-    outs[4].start()
-    outs[5].start()
-    for copy in outs:
-        copy.wait()
+    line_o[...] = line_step(lines2[place.bus], flows)
+    bal_o[...] = balance + total * (1.0 / float(B + S))
+    level_o[...] = level_step(prefixes[3].end(False))
+    ldual_o[...] = pad_l[0:NB, :]
     sends.finish()
 
 
@@ -569,11 +558,8 @@
         vm((NP, NP), BF16),
         vm((NP, NP), BF16),
         vm((NP, NP), F32),
-        vm((NB, HD), F32),
-        vm((LD, HD), F32),
         vm((4, Prefix.SLOTS, 1, NP), F32),
         dma((ARRAYS,)),
-        dma((6,)),
         dma,
         dma((16,)),
         dma,
@@ -594,7 +580,7 @@
         kernel,
         out_shape=tuple(pltpu.VMEM(shape.shape, F32) for shape in shapes),
         in_specs=[anywhere] * ARRAYS,
-        out_specs=[anywhere] * 6,
+        out_specs=[pl.BlockSpec(memory_space=pltpu.VMEM)] * 6,
         scratch_shapes=scratch,
         compiler_params=pltpu.CompilerParams(collective_id=0, has_side_effects=True, vmem_limit_bytes=56 * 1024 * 1024),
     )(

time: 79.1 us -> 77.4 us (0.979)
  Pallas kernels: 78.3 us -> 76.6 us
    pallas_call x1, Pallas kernels: 77.4 us -> 75.7 us  [body(): pl.pallas_call(kernel, out_shape=tuple((pltpu.VMEM(shape.shape, F32) for...]
where the time goes in v1:
time: 77.4 us; the launch traced here: 77.3 us
  Pallas kernels  76.6 us (99%)
    pallas_call x1, Pallas kernels, body(): pl.pallas_call(kernel, out_shape=tuple((pltpu.VMEM(shape.shape, F32) for...  75.7 us

profile of v1, /device:TPU:1, one launch (start us, length us, event | category | flops | bytes accessed | tf_op | source)
XLA Modules:
  0.0 77.3 jit_solution(5261147966481493644)
XLA Ops:
  0.6 75.7 %shard_map.181 = (f32[250,128]{1,0:T(8,128)S(1)}, f32[250,128]{1,0:T(8,128)S(1)}, f32[250,128]{1,0:T(8,128)S(1)}, f32[384,128]{1,0:T(8,128)S(1)}, f32[250,128]{1,0:T(8,128)S(1)}, /*index=5*/f32[1,128]{1,0:T(1,128)S(1)}) custom-call(f32[250,3072]{1,0:T(8,128)} %refs_0_.1, f32[250,128]{1,0:T(8,128)} %refs_1_.1, f32[250,128]{1,0:T(8,128)} %refs_2_.1, ...), custom_call_target="tpu_custom_call" | custom-call | tf_op jit(solution)/shard_map/pallas_call | solution.py:579
  76.4 0.9 %shard_map.182 = (f32[250,128]{1,0:T(8,128)}, f32[250,128]{1,0:T(8,128)}, f32[250,128]{1,0:T(8,128)}, f32[384,128]{1,0:T(8,128)}, f32[250,128]{1,0:T(8,128)}, /*index=5*/f32[1,128]{1,0:T(1,128)}) custom-call(f32[250,128]{1,0:T(8,128)S(1)} %get-tuple-element.18.refs_0_, f32[250,128]{1,0:T(8,128)S(1)} %get-tuple-element.19.refs_1_, ...), custom_call_target="tpu_custom_call" | custom-call | tf_op jit(solution)/shard_map/pallas_call | solution.py:602
